TPU v7x, 768 devices: a whole 4x8x12 slice. The times are simulated.
768 devices in a mesh: gx: 64 (over x, y, core), gy: 12 (over z).
Axes of the slice: x: 4, y: 8, z: 12, core: 2. Of those that a mesh axis runs over, the one named last changes fastest.
Arguments:
- block_input: bfloat16 [768, 40, 56, 256], P(('gx', 'gy')), may hold values from 0 to 6, as said below
- mid_first: bfloat16 [768, 40, 3584], P(('gx', 'gy')), may hold values from 0 to 6, as said below
- mid_second: bfloat16 [768, 40, 3584], P(('gx', 'gy')), may hold values from 0 to 18, as said below
- out_grad: bfloat16 [768, 40, 56, 256], P(('gx', 'gy')), may hold values from -6 to 6
- params: float32 [64, 1088], replicated, may hold values from -18 to 18
- velocity: float32 [64, 1088], P('gx'), may hold values from -1.8 to 1.8
Outputs:
- input_grad: bfloat16 [768, 40, 56, 256], P(('gx', 'gy'))
- new_velocity: float32 [64, 1088], P('gx')
- next_weights: float32 [64, 1088], replicated
Inputs may be any that keep to these rules, and one draw needn't show every extreme that they name: `block_input`: ReLU outputs: nonnegative, about half of the entries zero. `mid_first`: ReLU outputs: nonnegative, about half of the entries zero. `mid_second`: ReLU outputs: nonnegative, about half of the entries zero.
All inputs are finite; a program needn't handle non-finite values.
Results may differ from a plain program's by a relative error of at most 0.0074.
Values sent between devices are 32-bit elements; how exact they have to be, the bound alone decides.
A program may use at most 64 MiB of HBM per device.

v0:
```python
import math

import jax
import jax.numpy as jnp
from jax import lax
from jax.sharding import PartitionSpec as P

C_IN = 256
C_MID = 64


learn_rate = 0.5
momentum = 0.9
norm_eps = 1e-06


def tap_patches(field):
    img_height, img_width = (field.shape[0], field.shape[1])
    padded = jnp.pad(field, ((1, 1), (1, 1), (0, 0)))
    pieces = [
        padded[tap_row : tap_row + img_height, tap_col : tap_col + img_width]
        for tap_row in range(3)
        for tap_col in range(3)
    ]
    return jnp.concatenate(pieces, axis=2).reshape(img_height * img_width, 9 * field.shape[2])


def tap_sum(spread):
    img_height, img_width = (spread.shape[0], spread.shape[1])
    padded = jnp.pad(spread, ((1, 1), (1, 1), (0, 0), (0, 0)))
    result = jnp.zeros((img_height, img_width, spread.shape[3]), jnp.float32)
    for tap_row in range(3):
        for tap_col in range(3):
            result = (
                result
                + padded[
                    2 - tap_row : 2 - tap_row + img_height,
                    2 - tap_col : 2 - tap_col + img_width,
                    3 * tap_row + tap_col,
                ]
            )
    return result


def outer_sum(left, right):
    return lax.dot_general(
        left, right, (((0,), (0,)), ((), ())), preferred_element_type=jnp.float32
    )


def layer_squares(matrix):
    return jnp.stack(
        [
            jnp.sum(matrix[:, :C_IN] ** 2),
            jnp.sum(matrix[:, C_IN : C_IN + 9 * C_MID] ** 2),
            jnp.sum(matrix[:, C_IN + 9 * C_MID :] ** 2),
        ]
    )


def trust_columns(trust_ratio):
    return jnp.concatenate(
        [
            jnp.broadcast_to(trust_ratio[0], (C_IN,)),
            jnp.broadcast_to(trust_ratio[1], (9 * C_MID,)),
            jnp.broadcast_to(trust_ratio[2], (C_IN,)),
        ]
    )


def shards(block_input, mid_first, mid_second, out_grad, params, velocity):
    img_height, img_width = (block_input.shape[1], block_input.shape[2])
    pixels = img_height * img_width
    scale_one = 1.0 / math.sqrt(C_IN)
    scale_two = 1.0 / math.sqrt(9 * C_MID)
    scale_three = 1.0 / math.sqrt(C_MID)
    weights = params.astype(jnp.bfloat16)
    w_first = weights[:, :C_IN]
    w_second = weights[:, C_IN : C_IN + 9 * C_MID]
    w_third = weights[:, C_IN + 9 * C_MID :]
    input_flat = block_input.reshape(pixels, C_IN)
    out_flat = out_grad.reshape(pixels, C_IN)
    first_field = mid_first.reshape(img_height, img_width, C_MID)
    second_flat = mid_second.reshape(pixels, C_MID)
    back_second = (
        lax.dot_general(
            out_flat, w_third, (((1,), (1,)), ((), ())), preferred_element_type=jnp.float32
        )
        * scale_three
    )
    back_second = jnp.where(second_flat > 0, back_second, 0.0).astype(jnp.bfloat16)
    spread = jnp.dot(back_second, w_second, preferred_element_type=jnp.float32) * scale_two
    back_first = tap_sum(spread.reshape(img_height, img_width, 9, C_MID))
    back_first = (
        jnp.where(first_field > 0, back_first, 0.0).astype(jnp.bfloat16).reshape(pixels, C_MID)
    )
    input_grad = (
        out_flat.astype(jnp.float32)
        + scale_one * jnp.dot(back_first, w_first, preferred_element_type=jnp.float32)
    ).astype(jnp.bfloat16)
    patches = tap_patches(first_field)
    strips = lax.axis_size("gx") * lax.axis_size("gy")
    mean_factor = 1.0 / strips
    row_count = C_MID // lax.axis_size("gx")
    row_start = lax.axis_index("gx") * row_count
    blocks = [
        scale_one * outer_sum(back_first, input_flat),
        scale_two * outer_sum(back_second, patches),
        scale_three * outer_sum(second_flat, out_flat),
    ]
    own_grad = lax.psum_scatter(
        jnp.concatenate(blocks, axis=1) * mean_factor, "gx", scatter_dimension=0, tiled=True
    )
    own_grad = lax.psum(own_grad, "gy")
    grad_squares = lax.psum(layer_squares(own_grad), "gx")
    trust_ratio = jnp.sqrt(layer_squares(params)) / (jnp.sqrt(grad_squares) + norm_eps)
    own_params = lax.dynamic_slice_in_dim(params, row_start, row_count, 0)
    new_velocity = momentum * velocity + learn_rate * trust_columns(trust_ratio)[None, :] * own_grad
    new_shard = own_params - new_velocity
    next_weights = lax.all_gather(new_shard, "gx", axis=0, tiled=True)
    return (input_grad.reshape(1, img_height, img_width, C_IN), new_velocity, next_weights)


def solution(mesh):
    return jax.shard_map(
        shards,
        mesh=mesh,
        in_specs=(
            P(("gx", "gy"), None, None, None),
            P(("gx", "gy"), None, None),
            P(("gx", "gy"), None, None),
            P(("gx", "gy"), None, None, None),
            P(),
            P("gx", None),
        ),
        out_specs=(P(("gx", "gy"), None, None, None), P("gx", None), P()),
        check_vma=False,
    )
```

profile of v0, /device:TPU:1, one launch (start us, length us, event | category | flops | bytes accessed | tf_op | source)
XLA Modules:
  0.0 502.0 jit_solution(2025591029253069325)
XLA Ops:
  7.2 1.4 reshape.170
  8.7 2.2 reshape.175
  11.6 1.3 reshape.171
  14.9 2.2 copy.37
  17.1 6.7 %pad_slice_fusion.8 = (bf16[40,56,64]{1,0,2:T(8,128)(2,1)}, bf16[40,56,64]{1,0,2:T(8,128)(2,1)}, bf16[40,56,64]{1,0,2:T(8,128)(2,1)}, bf16[40,56,64]{1,0,2:T(8,1...) fusion(bf16[40,56,64]{1,0,2:T(8,128)(2,1)} %copy.37), kind=kLoop, calls=%fused_computation.26 | loop fusion | bytes 2580480 | tf_op jit(solution)/shard_map/slice | solution.py:21
  23.8 2.2 copy.53
  26.0 2.2 copy.47
  28.2 2.2 copy.48
  30.5 2.2 copy.49
  32.7 2.2 copy.50
  35.0 2.2 copy.51
  37.2 2.2 copy.52
  40.7 1.5 fusion.3
  42.2 3.2 convolution_multiply_fusion
  45.4 7.0 %concatenate.41 = bf16[2240,576]{1,0:T(8,128)(2,1)} concatenate(bf16[2240,64]{1,0:T(8,128)(2,1)} %bitcast.55, bf16[2240,64]{1,0:T(8,128)(2,1)} %bitcast.49, bf16[2240,64]{1,0:T(8,128)(2,1)} %bitcast.50, bf16[2240,64]{1,0:T(8,128)(2,1)} %bitcast.51, bf16[2240,64]{1,0:T(8,128)(2,1)S(1)} %reshape.170, bf16[2240,64]{1,0:T(8,128)(2,1)} %bitcast.52, bf16[2240,64]{1,0:T(8,128)(2,1)} %bitcast.53, ...), dimensions={1} | concatenate | bytes 5160960 | tf_op jit(solution)/shard_map/concatenate | solution.py:25
  52.5 3.1 convolution_multiply_fusion.3
  55.6 10.5 %reshape.172 = f32[40,56,9,64]{1,0,3,2:T(8,128)} reshape(f32[2240,576]{0,1:T(8,128)} %convolution_multiply_fusion) | data formatting | bytes 10321920 | tf_op jit(solution)/shard_map/reshape | solution.py:93
  66.1 6.5 %fusion.11 = bf16[40,56,1,64]{1,0,3,2:T(8,128)(2,1)S(1)} fusion(f32[40,56,9,64]{1,0,3,2:T(8,128)} %reshape.172), kind=kLoop, calls=%fused_computation.22 | loop fusion | flops 1290240 | bytes 13393920 | tf_op jit(solution)/shard_map/add | solution.py:35
  73.8 2.1 reshape.183
  75.9 1.8 select_convert_fusion.1
  77.8 2.1 convert_element_type.31
  79.9 2.0 convolution_multiply_fusion.5
  81.9 1.7 concatenate.42
  83.7 1.7 broadcast_multiply_fusion
  87.5 2.6 fusion.1
  92.8 198.3 %all-reduce.5.cloned.1.call-done = f32[64,1088]{1,0:T(8,128)} async-done(((f32[64,1088]{1,0:T(8,128)}), f32[64,1088]{1,0:T(8,128)}) %all-reduce.5.cloned.1.call-update) | async-done | bytes 278544
  291.1 1.4 constant_dynamic-slice_fusion
  292.5 20.0 %psum.14 = f32[1,1088]{1,0:T(1,128)S(1)} all-reduce(f32[1,1088]{1,0:T(1,128)S(1)} %constant_dynamic-slice_fusion), channel_id=1, replica_groups=mesh['gx'=64,'gy'=12] {'gy'}, use_global_device_ids=true, to_apply=%region_4.5 | all-reduce | flops 1088 | bytes 8704 | tf_op jit(solution)/shard_map/psum | solution.py:114
  313.9 2.0 pad_maximum_fusion
  315.8 129.6 %psum.15 = f32[3]{0:T(128)S(1)} all-reduce(f32[3]{0:T(128)S(1)} %pad_maximum_fusion), channel_id=1, replica_groups=mesh['gx'=64,'gy'=12] {'gx'}, use_global_device_ids=true, to_apply=%region_8.9 | all-reduce | flops 3 | bytes 24 | tf_op jit(solution)/shard_map/psum | solution.py:115
  445.5 2.0 fusion.20
  450.8 43.6 %all-gather = f32[64,1,1088]{2,1,0:T(1,128)S(1)} all-gather(f32[1,1,1088]{2,1,0:T(1,128)S(1)} %get-tuple-element.7), channel_id=1, replica_groups=mesh['gx'=64,'gy'=12] {'gx'}, dimensions={0}, use_global_device_ids=true | all-gather | bytes 282880 | tf_op jit(solution)/shard_map/all_gather | solution.py:120
  (33 shorter events, 15.3 us)
Async XLA Ops:
  7.2 72.7 %copy-start = (bf16[1,40,56,256]{3,2,1,0:T(8,128)(2,1)S(1)}, bf16[1,40,56,256]{3,2,1,0:T(8,128)(2,1)}, u32[]{:S(2)}) copy-start(bf16[1,40,56,256]{3,2,1,0:T(8,128)(2,1)} %param.6) | copy-start | bytes 3440644
  7.2 3.7 copy-start.2
  7.2 283.9 %all-reduce.5.cloned.1.call-start = ((), (), s32[]{:S(2)}) async-start(), calls=%async_computation | async-start | bytes 589824
  8.7 5.2 %copy-start.1 = (bf16[1,40,56,256]{3,2,1,0:T(8,128)(2,1)S(1)}, bf16[1,40,56,256]{3,2,1,0:T(8,128)(2,1)}, u32[]{:S(2)}) copy-start(bf16[1,40,56,256]{3,2,1,0:T(8,128)(2,1)} %param.9) | copy-start | bytes 3440644
  40.7 1.5 copy-start.4
  87.5 2.6 copy-start.3
  87.5 362.7 %copy-start.5 = (f32[1,1088]{1,0:T(1,128)S(1)}, f32[1,1088]{1,0:T(1,128)}, u32[]{:S(2)}) copy-start(f32[1,1088]{1,0:T(1,128)} %param.11) | copy-start | bytes 13060
Sparse Core Ops, SparseCore 0:
  85.5 205.5 all-reduce.4
where the time goes:
time: 504 us; the launch traced here: 502 us
  waiting for transfers between devices  198 us (39%)
  blocking collectives  193 us (38%)
  local copies, waits for them, and re-layouts  64.8 us (13%)
  other arithmetic  18 us (4%)
  between operations  14.1 us (3%)
  matrix products  13.5 us (3%)
    unnamed x2, waiting for transfers between devices  198 us
    psum x1, blocking collectives, shards(): grad_squares = lax.psum(layer_squares(own_grad), 'gx')  130 us
    all_gather x1, blocking collectives, shards(): next_weights = lax.all_gather(new_shard, 'gx', axis=0, tiled=True)  43.6 us
    concatenate x9, local copies, waits for them, and re-layouts, tap_patches(): jnp.concatenate(pieces, axis=2)  23.9 us
    psum x1, blocking collectives, shards(): own_grad = lax.psum(own_grad, 'gy')  20 us
    reshape x1, local copies, waits for them, and re-layouts, shards(): back_first = tap_sum(spread.reshape(img_height, img_width, 9, C_MID))  10.5 us
  transfers between devices with their start and end apart: 1, of which 1 were waited for; matrix products, arithmetic and copies ran while one was open for 1% of the time, Pallas kernels for 0%

commit v1 on v0

v1 whole, which is shorter than its diff:
```python
import functools
import math

import jax
import jax.numpy as jnp
from jax import lax
from jax.experimental import pallas as pl
from jax.experimental.pallas import tpu as pltpu
from jax.sharding import PartitionSpec as P

C_IN = 256
C_MID = 64
H_DEV = 40
W_IMG = 56
W_PAD = 64
K_ROW = 1088
K_PAD = 1152
PIXELS = H_DEV * W_PAD
ROWS_X = 4
ROWS_Y = 8
CORES = 2

H_CHUNK = 4
CHUNK = H_CHUNK * W_PAD
CHUNKS = H_DEV // H_CHUNK

learn_rate = 0.5
momentum = 0.9
norm_eps = 1e-06

F32 = jnp.float32
BF16 = jnp.bfloat16
MESH = pl.DeviceIdType.MESH

PART_W1 = (0, 256)
PART_W3 = (256, 256)
PART_W2 = (512, 640)


def dot(left, right, left_dim, right_dim):
    return lax.dot_general(
        left, right, (((left_dim,), (right_dim,)), ((), ())), preferred_element_type=F32
    )


def spread_pixels(fields, out):
    low = lax.broadcasted_iota(jnp.int32, (H_DEV, 128), 1) < 64
    for pair in range(W_IMG // 2):
        both = fields[:, 128 * pair : 128 * (pair + 1)].astype(F32)
        swapped = pltpu.roll(both, 64, 1)
        out[pl.ds(2 * pair, H_DEV, stride=W_PAD), :] = jnp.where(low, both, swapped)
        out[pl.ds(2 * pair + 1, H_DEV, stride=W_PAD), :] = jnp.where(low, swapped, both)
    zeros = jnp.zeros((W_PAD - W_IMG, 128), F32)
    for row in range(H_DEV):
        out[row * W_PAD + W_IMG : (row + 1) * W_PAD, :] = zeros


def padded_chunk(ref, chunk):
    values = ref[pl.ds(chunk * H_CHUNK, H_CHUNK)].astype(F32)
    zeros = jnp.zeros((H_CHUNK, W_PAD - W_IMG, C_IN), F32)
    return jnp.concatenate([values, zeros], axis=1).reshape(CHUNK, C_IN).astype(BF16)


def total(values):
    return jnp.sum(jnp.sum(values * values, axis=0, keepdims=True), axis=1, keepdims=True)


def kernel(
    size_x,
    size_y,
    size_z,
    x_hbm,
    first_hbm,
    second_hbm,
    grad_hbm,
    params,
    velocity,
    input_grad_hbm,
    new_velocity,
    next_weights,
    x_vmem,
    first_vmem,
    second_vmem,
    grad_vmem,
    input_grad_vmem,
    first_pix,
    second_pix,
    taps,
    back_first,
    w_first,
    w_second,
    w_third,
    sum_one,
    sum_two,
    sum_three,
    local,
    got_one,
    rows_two,
    got_two,
    got_three,
    rows_four,
    grads,
    velocities,
    velocity_flat,
    load_sem,
    store_sem,
    send_one,
    recv_one,
    send_two,
    recv_two,
    send_three,
    recv_three,
    send_four,
    recv_four,
    send_five,
    recv_five,
    send_vel,
    recv_vel,
):
    groups = size_x * CORES
    group_rows = C_MID // groups
    own_rows = group_rows // size_y
    strips = groups * size_y * size_z
    scale_one = 1.0 / math.sqrt(C_IN)
    scale_two = 1.0 / math.sqrt(9 * C_MID)
    scale_three = 1.0 / math.sqrt(C_MID)
    mean_factor = 1.0 / strips

    gx = lax.axis_index("gx")
    my_z = lax.axis_index("gy")
    my_core = lax.rem(gx, CORES)
    my_y = lax.rem(gx // CORES, size_y)
    my_x = gx // (CORES * size_y)
    my_group = my_x * CORES + my_core

    def group_peer(step):
        peer = lax.rem(my_group + step, groups)
        index = ((peer // CORES) * size_y + my_y) * CORES + lax.rem(peer, CORES)
        return peer, (index, my_z)

    def y_peer(step):
        peer = lax.rem(my_y + step, size_y)
        return peer, ((my_x * size_y + peer) * CORES + my_core, my_z)

    def z_peer(step):
        peer = lax.rem(my_z + step, size_z)
        return peer, (gx, peer)

    axes = ((groups, group_peer), (size_y, y_peer), (size_z, z_peer))

    loads = []
    for index, (src, dst) in enumerate(
        (
            (second_hbm, second_vmem),
            (grad_hbm, grad_vmem),
            (first_hbm, first_vmem),
            (x_hbm, x_vmem),
        )
    ):
        load = pltpu.make_async_copy(src.at[0], dst, load_sem.at[index])
        load.start()
        loads.append(load)

    barrier = pltpu.get_barrier_semaphore()
    for size, peer_of in axes:
        for step in range(1, size):
            pl.semaphore_signal(barrier, inc=1, device_id=peer_of(step)[1], device_id_type=MESH)

    weights = params[...].astype(BF16)
    w_first[...] = weights[:, :C_IN]
    for tap_row in range(3):
        start = C_IN + 3 * C_MID * tap_row
        w_second[C_MID * tap_row : C_MID * (tap_row + 1), :] = weights[:, start : start + 3 * C_MID]
        w_third[C_MID * tap_row : C_MID * (tap_row + 1), :] = weights[:, C_IN + 9 * C_MID :]

    sum_one[...] = jnp.zeros_like(sum_one)
    sum_two[...] = jnp.zeros_like(sum_two)
    sum_three[...] = jnp.zeros_like(sum_three)
    no_taps = jnp.zeros((W_PAD, C_MID), BF16)
    taps[W_PAD : 2 * W_PAD, 2 * C_MID :] = no_taps
    taps[PIXELS : PIXELS + W_PAD, :C_MID] = no_taps

    loads[0].wait()
    spread_pixels(second_vmem, second_pix)
    loads[1].wait()

    def step_second(chunk, carry):
        start = pl.multiple_of(chunk * CHUNK, CHUNK)
        out_grad = padded_chunk(grad_vmem, chunk)
        second = second_pix[pl.ds(start, CHUNK), :]
        back = dot(out_grad, w_third[...], 1, 1) * scale_three
        both = jnp.where(second > 0, back[:, :128], 0.0).astype(BF16)
        last = jnp.where(second[:, :C_MID] > 0, back[:, 128:], 0.0).astype(BF16)
        taps[pl.ds(start, CHUNK), :C_MID] = both[:, :C_MID]
        taps[pl.ds(start + W_PAD, CHUNK), C_MID : 2 * C_MID] = both[:, C_MID:]
        taps[pl.ds(start + 2 * W_PAD, CHUNK), 2 * C_MID :] = last
        sum_three[...] += dot(second[:, :C_MID].astype(BF16), out_grad, 0, 0)
        return carry

    lax.fori_loop(0, CHUNKS, step_second, 0)

    def place(columns, values):
        local[:, :, columns : columns + values.shape[1]] = values.reshape(
            groups, group_rows, values.shape[1]
        )

    def part_copy(index, columns, peer, slot, device):
        return pltpu.make_async_remote_copy(
            src_ref=local.at[peer, :, pl.ds(*columns)],
            dst_ref=got_one.at[slot, :, pl.ds(*columns)],
            send_sem=send_one.at[index, peer],
            recv_sem=recv_one.at[index, slot],
            device_id=device,
            device_id_type=MESH,
        )

    parts = (PART_W3, PART_W2, PART_W1)

    def send_part(index):
        for step in range(1, groups):
            peer, device = group_peer(step)
            part_copy(index, parts[index], peer, my_group, device).start()

    def velocity_copy(kind, ref, slot, device):
        return pltpu.make_async_remote_copy(
            src_ref=ref,
            dst_ref=ref,
            send_sem=send_vel.at[kind, slot[0]],
            recv_sem=recv_vel.at[kind, slot[1]],
            device_id=device,
            device_id_type=MESH,
        )

    place(PART_W3[0], sum_three[...] * (scale_three * mean_factor))
    velocities[my_x, my_y, my_core] = velocity[...]
    pl.semaphore_wait(barrier, sum(size - 1 for size, _ in axes))
    send_part(0)
    for step in range(1, size_y):
        peer, device = y_peer(step)
        velocity_copy(0, velocities.at[my_x, my_y, my_core], (peer, my_y), device).start()

    loads[2].wait()
    spread_pixels(first_vmem, first_pix)
    loads[3].wait()

    low = lax.broadcasted_iota(jnp.int32, (CHUNK, 128), 1) < 64

    def step_first(chunk, carry):
        start = pl.multiple_of(chunk * CHUNK, CHUNK)
        first = first_pix[pl.ds(start, CHUNK), :]
        tap = taps[pl.ds(start + W_PAD, CHUNK), :]
        shifted = jnp.concatenate(
            [
                jnp.where(low, pltpu.roll(first, 1, 0), first),
                pltpu.roll(first, CHUNK - 1, 0)[:, :C_MID],
            ],
            axis=1,
        ).astype(BF16)
        sum_two[...] += dot(tap, shifted, 0, 0)
        spread = dot(tap, w_second[...], 1, 0)
        mixed = (
            pltpu.roll(spread[:, :128], CHUNK - 1, 0)[:, :C_MID]
            + spread[:, C_MID : 2 * C_MID]
            + pltpu.roll(spread[:, 128:], 1, 0)
        ) * scale_two
        back = jnp.where(first[:, :C_MID] > 0, mixed, 0.0).astype(BF16)
        back_first[pl.ds(start, CHUNK), :] = back
        sum_one[...] += dot(back, padded_chunk(x_vmem, chunk), 0, 0)
        return carry

    lax.fori_loop(0, CHUNKS, step_first, 0)

    for tap_row in range(3):
        place(
            PART_W2[0] + 3 * C_MID * tap_row,
            sum_two[C_MID * tap_row : C_MID * (tap_row + 1), :] * (scale_two * mean_factor),
        )
    local[:, :, K_ROW:] = jnp.zeros((groups, group_rows, K_PAD - K_ROW), F32)
    place(PART_W1[0], sum_one[...] * (scale_one * mean_factor))
    send_part(1)
    send_part(2)

    for step in range(1, size_y):
        peer, device = y_peer(step)
        velocity_copy(0, velocities.at[my_x, peer, my_core], (peer, peer), device).wait_recv()
    for step in range(1, groups):
        peer, device = group_peer(step)
        velocity_copy(1, velocities.at[my_x, :, my_core], (peer, my_group), device).start()

    def step_input(chunk, carry):
        start = pl.multiple_of(chunk * CHUNK, CHUNK)
        rise = dot(back_first[pl.ds(start, CHUNK), :], w_first[...], 1, 0) * scale_one
        rise = rise.reshape(H_CHUNK, W_PAD, C_IN)[:, :W_IMG]
        rows = pl.ds(chunk * H_CHUNK, H_CHUNK)
        input_grad_vmem[rows] = (grad_vmem[rows].astype(F32) + rise).astype(BF16)
        return carry

    lax.fori_loop(0, CHUNKS, step_input, 0)
    store = pltpu.make_async_copy(input_grad_vmem, input_grad_hbm.at[0], store_sem)
    store.start()

    block = local[my_group]
    for step in range(1, groups):
        peer, device = group_peer(step)
        for index in range(3):
            part_copy(index, parts[index], peer, peer, device).wait_recv()
        block = block + got_one[peer]
    for index in range(size_y):
        rows_two[index] = block[index * own_rows : (index + 1) * own_rows]

    def two_copy(peer, slot, device):
        return pltpu.make_async_remote_copy(
            src_ref=rows_two.at[peer],
            dst_ref=got_two.at[slot],
            send_sem=send_two.at[peer],
            recv_sem=recv_two.at[slot],
            device_id=device,
            device_id_type=MESH,
        )

    for step in range(1, size_y):
        peer, device = y_peer(step)
        two_copy(peer, my_y, device).start()
    row = rows_two[my_y]
    for step in range(1, size_y):
        peer, device = y_peer(step)
        two_copy(peer, peer, device).wait_recv()
        row = row + got_two[peer]

    def three_copy(slot, peer, device):
        return pltpu.make_async_remote_copy(
            src_ref=got_three.at[slot],
            dst_ref=got_three.at[slot],
            send_sem=send_three.at[peer],
            recv_sem=recv_three.at[slot],
            device_id=device,
            device_id_type=MESH,
        )

    got_three[my_z] = row
    for step in range(1, size_z):
        peer, device = z_peer(step)
        three_copy(my_z, peer, device).start()
    for step in range(1, size_z):
        peer, device = z_peer(step)
        three_copy(peer, peer, device).wait_recv()
    row = got_three[0]
    for index in range(1, size_z):
        row = row + got_three[index]

    def four_copy(slot, peer, device):
        return pltpu.make_async_remote_copy(
            src_ref=rows_four.at[slot],
            dst_ref=rows_four.at[slot],
            send_sem=send_four.at[peer],
            recv_sem=recv_four.at[slot],
            device_id=device,
            device_id_type=MESH,
        )

    rows_four[my_y] = row
    for step in range(1, size_y):
        peer, device = y_peer(step)
        four_copy(my_y, peer, device).start()

    for step in range(1, groups):
        peer, device = group_peer(step)
        other = velocities.at[peer // CORES, :, lax.rem(peer, CORES)]
        velocity_copy(1, other, (peer, peer), device).wait_recv()
    for at_x in range(size_x):
        for at_y in range(size_y):
            for at_core in range(CORES):
                index = (at_x * size_y + at_y) * CORES + at_core
                velocity_flat[index * own_rows : (index + 1) * own_rows, :] = velocities[
                    at_x, at_y, at_core
                ]
    bounds = (
        (0, C_IN, PART_W1[0]),
        (C_IN, C_IN + 9 * C_MID, PART_W2[0]),
        (C_IN + 9 * C_MID, K_ROW, PART_W3[0]),
    )
    weight_norms = [jnp.sqrt(total(params[:, low_end:high_end])) for low_end, high_end, _ in bounds]

    for step in range(1, size_y):
        peer, device = y_peer(step)
        four_copy(peer, peer, device).wait_recv()
    for index in range(size_y):
        grads[my_group, index * own_rows : (index + 1) * own_rows, :] = rows_four[index]

    def five_copy(slot, peer, device):
        return pltpu.make_async_remote_copy(
            src_ref=grads.at[slot],
            dst_ref=grads.at[slot],
            send_sem=send_five.at[peer],
            recv_sem=recv_five.at[slot],
            device_id=device,
            device_id_type=MESH,
        )

    for step in range(1, groups):
        peer, device = group_peer(step)
        five_copy(my_group, peer, device).start()
    for step in range(1, groups):
        peer, device = group_peer(step)
        five_copy(peer, peer, device).wait_recv()

    for (low_end, high_end, column), weight_norm in zip(bounds, weight_norms):
        grad = grads[:, :, column : column + high_end - low_end].reshape(
            C_MID, high_end - low_end
        )
        rate = learn_rate * (weight_norm / (jnp.sqrt(total(grad)) + norm_eps))
        fresh = momentum * velocity_flat[:, low_end:high_end] + rate * grad
        velocity_flat[:, low_end:high_end] = fresh
        next_weights[:, low_end:high_end] = params[:, low_end:high_end] - fresh
    new_velocity[...] = velocity_flat[pl.ds(gx * own_rows, own_rows), :]

    for step in range(1, groups):
        peer, device = group_peer(step)
        for index in range(3):
            part_copy(index, parts[index], peer, my_group, device).wait_send()
        velocity_copy(1, velocities.at[my_x, :, my_core], (peer, my_group), device).wait_send()
        five_copy(my_group, peer, device).wait_send()
    for step in range(1, size_y):
        peer, device = y_peer(step)
        velocity_copy(0, velocities.at[my_x, my_y, my_core], (peer, my_y), device).wait_send()
        two_copy(peer, my_y, device).wait_send()
        four_copy(my_y, peer, device).wait_send()
    for step in range(1, size_z):
        peer, device = z_peer(step)
        three_copy(my_z, peer, device).wait_send()
    store.wait()


def shards(size_x, size_y, size_z, block_input, mid_first, mid_second, out_grad, params, velocity):
    groups = size_x * CORES
    group_rows = C_MID // groups
    own_rows = group_rows // size_y
    dma = pltpu.SemaphoreType.DMA
    return pl.pallas_call(
        functools.partial(kernel, size_x, size_y, size_z),
        out_shape=(
            jax.ShapeDtypeStruct((1, H_DEV, W_IMG, C_IN), BF16),
            jax.ShapeDtypeStruct((own_rows, K_ROW), F32),
            jax.ShapeDtypeStruct((C_MID, K_ROW), F32),
        ),
        in_specs=[pl.BlockSpec(memory_space=pl.ANY)] * 4
        + [pl.BlockSpec(memory_space=pltpu.VMEM)] * 2,
        out_specs=(
            pl.BlockSpec(memory_space=pl.ANY),
            pl.BlockSpec(memory_space=pltpu.VMEM),
            pl.BlockSpec(memory_space=pltpu.VMEM),
        ),
        scratch_shapes=[
            pltpu.VMEM((H_DEV, W_IMG, C_IN), BF16),
            pltpu.VMEM((H_DEV, W_IMG * C_MID), BF16),
            pltpu.VMEM((H_DEV, W_IMG * C_MID), BF16),
            pltpu.VMEM((H_DEV, W_IMG, C_IN), BF16),
            pltpu.VMEM((H_DEV, W_IMG, C_IN), BF16),
            pltpu.VMEM((PIXELS, 128), F32),
            pltpu.VMEM((PIXELS, 128), F32),
            pltpu.VMEM((PIXELS + 2 * W_PAD, 3 * C_MID), BF16),
            pltpu.VMEM((PIXELS, C_MID), BF16),
            pltpu.VMEM((C_MID, C_IN), BF16),
            pltpu.VMEM((3 * C_MID, 3 * C_MID), BF16),
            pltpu.VMEM((3 * C_MID, C_IN), BF16),
            pltpu.VMEM((C_MID, C_IN), F32),
            pltpu.VMEM((3 * C_MID, 3 * C_MID), F32),
            pltpu.VMEM((C_MID, C_IN), F32),
            pltpu.VMEM((groups, group_rows, K_PAD), F32),
            pltpu.VMEM((groups, group_rows, K_PAD), F32),
            pltpu.VMEM((size_y, own_rows, K_PAD), F32),
            pltpu.VMEM((size_y, own_rows, K_PAD), F32),
            pltpu.VMEM((size_z, own_rows, K_PAD), F32),
            pltpu.VMEM((size_y, own_rows, K_PAD), F32),
            pltpu.VMEM((groups, group_rows, K_PAD), F32),
            pltpu.VMEM((size_x, size_y, CORES, own_rows, K_ROW), F32),
            pltpu.VMEM((C_MID, K_ROW), F32),
            dma((4,)),
            dma,
            dma((3, groups)),
            dma((3, groups)),
            dma((size_y,)),
            dma((size_y,)),
            dma((size_z,)),
            dma((size_z,)),
            dma((size_y,)),
            dma((size_y,)),
            dma((groups,)),
            dma((groups,)),
            dma((2, max(groups, size_y))),
            dma((2, max(groups, size_y))),
        ],
        compiler_params=pltpu.CompilerParams(
            collective_id=0, has_side_effects=True, vmem_limit_bytes=62 * 1024 * 1024
        ),
        name="bottleneck_backward",
    )(block_input, mid_first, mid_second, out_grad, params, velocity)


def solution(mesh):
    return jax.shard_map(
        functools.partial(shards, ROWS_X, ROWS_Y, mesh.shape["gy"]),
        mesh=mesh,
        in_specs=(
            P(("gx", "gy"), None, None, None),
            P(("gx", "gy"), None, None),
            P(("gx", "gy"), None, None),
            P(("gx", "gy"), None, None, None),
            P(),
            P("gx", None),
        ),
        out_specs=(P(("gx", "gy"), None, None, None), P("gx", None), P()),
        check_vma=False,
    )
```

time: 504 us -> 57.4 us (0.11)
  waiting for transfers between devices: 198 us -> 0 us
  blocking collectives: 193 us -> 0 us
  local copies, waits for them, and re-layouts: 64.8 us -> 3.69 us
  Pallas kernels: 0 us -> 52.9 us
  other arithmetic: 18 us -> 0 us
  matrix products: 13.5 us -> 0 us
  between operations: 14.1 us -> 0.66 us
    unnamed x2 -> x0, waiting for transfers between devices: 198 us -> none
    psum x2 -> x0, blocking collectives: 150 us -> none  [the longest x1 130 us: shards(): grad_squares = lax.psum(layer_squares(own_grad), 'gx')]
    pallas_call x0 -> x1, Pallas kernels: none -> 52.9 us  [shards(): pl.pallas_call(functools.partial(kernel, size_x, size_y, size_z), out_sha...]
    all_gather x1 -> x0, blocking collectives: 43.6 us -> none  [shards(): next_weights = lax.all_gather(new_shard, 'gx', axis=0, tiled=True)]
    concatenate x11 -> x0, local copies, waits for them, and re-layouts: 25.8 us -> none  [the longest x9 23.9 us: tap_patches(): jnp.concatenate(pieces, axis=2)]
    reshape x7 -> x0, local copies, waits for them, and re-layouts: 19.6 us -> none  [the longest x1 10.5 us: shards(): back_first = tap_sum(spread.reshape(img_height, img_width, 9, C_MID))]
    dot_general x6 -> x0, matrix products: 13.5 us -> none  [the longest x3 6.13 us: outer_sum(): lax.dot_general(left, right, (((0,), (0,)), ((), ())), preferred_element_...]
    slice x2 -> x0, local copies, waits for them, and re-layouts: 7.34 us -> none  [the longest x1 6.67 us: tap_patches(): padded[tap_row:tap_row + img_height, tap_col:tap_col + img_width]]
  transfers between devices with their start and end apart: 1 -> 0, of which waited for: 1 -> 0; matrix products, arithmetic and copies ran while one was open for 1% -> 0% of each run, Pallas kernels for 0% -> 0%
where the time goes in v1:
time: 57.4 us; the launch traced here: 57.3 us
  Pallas kernels  52.9 us (92%)
  local copies, waits for them, and re-layouts  3.69 us (6%)
  between operations  0.66 us (1%)
    pallas_call x1, Pallas kernels, shards(): pl.pallas_call(functools.partial(kernel, size_x, size_y, size_z), out_sha...  52.9 us
    unnamed x7, local copies, waits for them, and re-layouts  3.69 us

profile of v1, /device:TPU:1, one launch (start us, length us, event | category | flops | bytes accessed | tf_op | source)
XLA Modules:
  0.0 57.3 jit_solution(8293689896756260454)
XLA Ops:
  0.6 52.9 %bottleneck_backward.1 = (bf16[1,40,56,256]{3,2,1,0:T(8,128)(2,1)}, f32[1,1088]{1,0:T(1,128)}, f32[64,1088]{1,0:T(8,128)}) custom-call(bf16[1,40,56,256]{3,2,1,0:T(8,128)(2,1)} %x_hbm.1, bf16[1,40,3584]{2,1,0:T(8,128)(2,1)} %first_hbm.1, bf16[1,40,3584]{2,1,0:T(8,128)(2,1)} %second_hbm.1, bf16[1,40,56,256]{3,2,1,0:T(8,128)(2,1)} %grad_hbm.1, ...), custom_call_target="tpu_custom_call" | custom-call | tf_op jit(solution)/shard_map/bottleneck_backward/pallas_call | solution.py:439
  53.5 0.0 copy-start.1
  53.5 0.0 copy-start
  53.6 2.4 %copy.12 = bf16[1,40,56,256]{3,2,1,0:T(8,128)(2,1)} copy(bf16[1,40,56,256]{3,2,1,0:T(8,128)(2,1)} %get-tuple-element.6) | data formatting | bytes 2293760
  55.9 0.0 copy-done.1
  55.9 0.6 %copy.13 = f32[1,1088]{1,0:T(1,128)} copy(f32[1,1088]{1,0:T(1,128)S(1)} %copy-done.1) | data formatting | bytes 8704
  56.5 0.0 copy-done
  56.5 0.7 %copy.14 = f32[64,1088]{1,0:T(8,128)} copy(f32[64,1088]{1,0:T(8,128)S(1)} %copy-done) | data formatting | bytes 557056
Async XLA Ops:
  53.5 2.4 %copy-start.1 = (f32[1,1088]{1,0:T(1,128)S(1)}, f32[1,1088]{1,0:T(1,128)}, u32[]{:S(2)}) copy-start(f32[1,1088]{1,0:T(1,128)} %get-tuple-element.7) | copy-start | bytes 13060
  53.5 3.0 %copy-start = (f32[64,1088]{1,0:T(8,128)S(1)}, f32[64,1088]{1,0:T(8,128)}, u32[]{:S(2)}) copy-start(f32[64,1088]{1,0:T(8,128)} %get-tuple-element.8) | copy-start | bytes 835588

commit v2 on v1

--- a/solution.py
+++ b/solution.py
@@ -20,7 +20,7 @@
 ROWS_Y = 8
 CORES = 2
 
-H_CHUNK = 4
+H_CHUNK = 8
 CHUNK = H_CHUNK * W_PAD
 CHUNKS = H_DEV // H_CHUNK
 
@@ -32,9 +32,10 @@
 BF16 = jnp.bfloat16
 MESH = pl.DeviceIdType.MESH
 
-PART_W1 = (0, 256)
-PART_W3 = (256, 256)
-PART_W2 = (512, 640)
+AT_W3 = 0
+AT_W1 = 256
+AT_W2 = 512
+PARTS = ((0, K_PAD),)
 
 
 def dot(left, right, left_dim, right_dim):
@@ -56,9 +57,14 @@
 
 
 def padded_chunk(ref, chunk):
-    values = ref[pl.ds(chunk * H_CHUNK, H_CHUNK)].astype(F32)
+    values = ref[chunk * H_CHUNK : (chunk + 1) * H_CHUNK].astype(F32)
     zeros = jnp.zeros((H_CHUNK, W_PAD - W_IMG, C_IN), F32)
     return jnp.concatenate([values, zeros], axis=1).reshape(CHUNK, C_IN).astype(BF16)
+
+
+def each_chunk(step):
+    for chunk in range(CHUNKS):
+        step(chunk)
 
 
 def total(values):
@@ -73,16 +79,17 @@
     first_hbm,
     second_hbm,
     grad_hbm,
-    params,
-    velocity,
-    input_grad_hbm,
+    params_hbm,
+    velocity_hbm,
+    input_grad,
     new_velocity,
     next_weights,
     x_vmem,
     first_vmem,
     second_vmem,
     grad_vmem,
-    input_grad_vmem,
+    params,
+    velocity,
     first_pix,
     second_pix,
     taps,
@@ -103,7 +110,6 @@
     velocities,
     velocity_flat,
     load_sem,
-    store_sem,
     send_one,
     recv_one,
     send_two,
@@ -126,6 +132,21 @@
     scale_three = 1.0 / math.sqrt(C_MID)
     mean_factor = 1.0 / strips
 
+    def rows_of(chunk):
+        return pl.ds(chunk * H_CHUNK, H_CHUNK)
+
+    def load(src, dst, slot):
+        copy = pltpu.make_async_copy(src, dst, load_sem.at[slot])
+        copy.start()
+        return copy
+
+    load_params = load(params_hbm, params, 0)
+    load_second = load(second_hbm.at[0], second_vmem, 1)
+    load_grad = load(grad_hbm.at[0], grad_vmem, 2)
+    load_first = load(first_hbm.at[0], first_vmem, 3)
+    load_x = load(x_hbm.at[0], x_vmem, 4)
+    load_velocity = load(velocity_hbm, velocity, 5)
+
     gx = lax.axis_index("gx")
     my_z = lax.axis_index("gy")
     my_core = lax.rem(gx, CORES)
@@ -133,39 +154,30 @@
     my_x = gx // (CORES * size_y)
     my_group = my_x * CORES + my_core
 
-    def group_peer(step):
-        peer = lax.rem(my_group + step, groups)
-        index = ((peer // CORES) * size_y + my_y) * CORES + lax.rem(peer, CORES)
-        return peer, (index, my_z)
-
-    def y_peer(step):
-        peer = lax.rem(my_y + step, size_y)
-        return peer, ((my_x * size_y + peer) * CORES + my_core, my_z)
-
-    def z_peer(step):
-        peer = lax.rem(my_z + step, size_z)
-        return peer, (gx, peer)
-
-    axes = ((groups, group_peer), (size_y, y_peer), (size_z, z_peer))
-
-    loads = []
-    for index, (src, dst) in enumerate(
-        (
-            (second_hbm, second_vmem),
-            (grad_hbm, grad_vmem),
-            (first_hbm, first_vmem),
-            (x_hbm, x_vmem),
-        )
-    ):
-        load = pltpu.make_async_copy(src.at[0], dst, load_sem.at[index])
-        load.start()
-        loads.append(load)
+    def wrap(index, size):
+        return jnp.where(index >= size, index - size, index)
+
+    group_peers = []
+    for step in range(size_x):
+        peer_x = wrap(my_x + step, size_x)
+        for core in (my_core, 1 - my_core) if step else (1 - my_core,):
+            index = (peer_x * size_y + my_y) * CORES + core
+            group_peers.append((peer_x * CORES + core, (index, my_z), peer_x, core))
+    y_peers = []
+    for step in range(1, size_y):
+        peer = wrap(my_y + step, size_y)
+        y_peers.append((peer, ((my_x * size_y + peer) * CORES + my_core, my_z)))
+    z_peers = []
+    for step in range(1, size_z):
+        peer = wrap(my_z + step, size_z)
+        z_peers.append((peer, (gx, peer)))
 
     barrier = pltpu.get_barrier_semaphore()
-    for size, peer_of in axes:
-        for step in range(1, size):
-            pl.semaphore_signal(barrier, inc=1, device_id=peer_of(step)[1], device_id_type=MESH)
-
+    everyone = [peer[1] for peer in group_peers + y_peers + z_peers]
+    for device in everyone:
+        pl.semaphore_signal(barrier, inc=1, device_id=device, device_id_type=MESH)
+
+    load_params.wait()
     weights = params[...].astype(BF16)
     w_first[...] = weights[:, :C_IN]
     for tap_row in range(3):
@@ -180,12 +192,21 @@
     taps[W_PAD : 2 * W_PAD, 2 * C_MID :] = no_taps
     taps[PIXELS : PIXELS + W_PAD, :C_MID] = no_taps
 
-    loads[0].wait()
+    def velocity_copy(kind, ref, slot, device):
+        return pltpu.make_async_remote_copy(
+            src_ref=ref,
+            dst_ref=ref,
+            send_sem=send_vel.at[kind, slot[0]],
+            recv_sem=recv_vel.at[kind, slot[1]],
+            device_id=device,
+            device_id_type=MESH,
+        )
+
+    load_second.wait()
     spread_pixels(second_vmem, second_pix)
-    loads[1].wait()
-
-    def step_second(chunk, carry):
-        start = pl.multiple_of(chunk * CHUNK, CHUNK)
+
+    def step_second(chunk):
+        start = chunk * CHUNK
         out_grad = padded_chunk(grad_vmem, chunk)
         second = second_pix[pl.ds(start, CHUNK), :]
         back = dot(out_grad, w_third[...], 1, 1) * scale_three
@@ -195,9 +216,9 @@
         taps[pl.ds(start + W_PAD, CHUNK), C_MID : 2 * C_MID] = both[:, C_MID:]
         taps[pl.ds(start + 2 * W_PAD, CHUNK), 2 * C_MID :] = last
         sum_three[...] += dot(second[:, :C_MID].astype(BF16), out_grad, 0, 0)
-        return carry
-
-    lax.fori_loop(0, CHUNKS, step_second, 0)
+
+    load_grad.wait()
+    each_chunk(step_second)
 
     def place(columns, values):
         local[:, :, columns : columns + values.shape[1]] = values.reshape(
@@ -214,39 +235,19 @@
             device_id_type=MESH,
         )
 
-    parts = (PART_W3, PART_W2, PART_W1)
-
     def send_part(index):
-        for step in range(1, groups):
-            peer, device = group_peer(step)
-            part_copy(index, parts[index], peer, my_group, device).start()
-
-    def velocity_copy(kind, ref, slot, device):
-        return pltpu.make_async_remote_copy(
-            src_ref=ref,
-            dst_ref=ref,
-            send_sem=send_vel.at[kind, slot[0]],
-            recv_sem=recv_vel.at[kind, slot[1]],
-            device_id=device,
-            device_id_type=MESH,
-        )
-
-    place(PART_W3[0], sum_three[...] * (scale_three * mean_factor))
-    velocities[my_x, my_y, my_core] = velocity[...]
-    pl.semaphore_wait(barrier, sum(size - 1 for size, _ in axes))
-    send_part(0)
-    for step in range(1, size_y):
-        peer, device = y_peer(step)
-        velocity_copy(0, velocities.at[my_x, my_y, my_core], (peer, my_y), device).start()
-
-    loads[2].wait()
+        for peer, device, peer_x, peer_core in group_peers:
+            part_copy(index, PARTS[index], peer, my_group, device).start()
+
+    place(AT_W3, sum_three[...] * (scale_three * mean_factor))
+
+    load_first.wait()
     spread_pixels(first_vmem, first_pix)
-    loads[3].wait()
 
     low = lax.broadcasted_iota(jnp.int32, (CHUNK, 128), 1) < 64
 
-    def step_first(chunk, carry):
-        start = pl.multiple_of(chunk * CHUNK, CHUNK)
+    def step_first(chunk):
+        start = chunk * CHUNK
         first = first_pix[pl.ds(start, CHUNK), :]
         tap = taps[pl.ds(start + W_PAD, CHUNK), :]
         shifted = jnp.concatenate(
@@ -266,44 +267,37 @@
         back = jnp.where(first[:, :C_MID] > 0, mixed, 0.0).astype(BF16)
         back_first[pl.ds(start, CHUNK), :] = back
         sum_one[...] += dot(back, padded_chunk(x_vmem, chunk), 0, 0)
-        return carry
-
-    lax.fori_loop(0, CHUNKS, step_first, 0)
+
+    load_x.wait()
+    each_chunk(step_first)
 
     for tap_row in range(3):
         place(
-            PART_W2[0] + 3 * C_MID * tap_row,
+            AT_W2 + 3 * C_MID * tap_row,
             sum_two[C_MID * tap_row : C_MID * (tap_row + 1), :] * (scale_two * mean_factor),
         )
     local[:, :, K_ROW:] = jnp.zeros((groups, group_rows, K_PAD - K_ROW), F32)
-    place(PART_W1[0], sum_one[...] * (scale_one * mean_factor))
-    send_part(1)
-    send_part(2)
-
-    for step in range(1, size_y):
-        peer, device = y_peer(step)
-        velocity_copy(0, velocities.at[my_x, peer, my_core], (peer, peer), device).wait_recv()
-    for step in range(1, groups):
-        peer, device = group_peer(step)
-        velocity_copy(1, velocities.at[my_x, :, my_core], (peer, my_group), device).start()
-
-    def step_input(chunk, carry):
-        start = pl.multiple_of(chunk * CHUNK, CHUNK)
+    place(AT_W1, sum_one[...] * (scale_one * mean_factor))
+    load_velocity.wait()
+    velocities[my_x, my_y, my_core] = velocity[...]
+    pl.semaphore_wait(barrier, len(everyone))
+    send_part(0)
+    for peer, device in y_peers:
+        velocity_copy(0, velocities.at[my_x, my_y, my_core], (peer, my_y), device).start()
+
+    def step_input(chunk):
+        start = chunk * CHUNK
         rise = dot(back_first[pl.ds(start, CHUNK), :], w_first[...], 1, 0) * scale_one
         rise = rise.reshape(H_CHUNK, W_PAD, C_IN)[:, :W_IMG]
-        rows = pl.ds(chunk * H_CHUNK, H_CHUNK)
-        input_grad_vmem[rows] = (grad_vmem[rows].astype(F32) + rise).astype(BF16)
-        return carry
-
-    lax.fori_loop(0, CHUNKS, step_input, 0)
-    store = pltpu.make_async_copy(input_grad_vmem, input_grad_hbm.at[0], store_sem)
-    store.start()
+        rows = rows_of(chunk)
+        input_grad[0, rows] = (grad_vmem[rows].astype(F32) + rise).astype(BF16)
+
+    each_chunk(step_input)
 
     block = local[my_group]
-    for step in range(1, groups):
-        peer, device = group_peer(step)
-        for index in range(3):
-            part_copy(index, parts[index], peer, peer, device).wait_recv()
+    for peer, device, peer_x, peer_core in group_peers:
+        for index in range(len(PARTS)):
+            part_copy(index, PARTS[index], peer, peer, device).wait_recv()
         block = block + got_one[peer]
     for index in range(size_y):
         rows_two[index] = block[index * own_rows : (index + 1) * own_rows]
@@ -318,12 +312,16 @@
             device_id_type=MESH,
         )
 
-    for step in range(1, size_y):
-        peer, device = y_peer(step)
+    for peer, device in y_peers:
         two_copy(peer, my_y, device).start()
+
+    for peer, device in y_peers:
+        velocity_copy(0, velocities.at[my_x, peer, my_core], (peer, peer), device).wait_recv()
+    for peer, device, peer_x, peer_core in group_peers:
+        velocity_copy(1, velocities.at[my_x, :, my_core], (peer, my_group), device).start()
+
     row = rows_two[my_y]
-    for step in range(1, size_y):
-        peer, device = y_peer(step)
+    for peer, device in y_peers:
         two_copy(peer, peer, device).wait_recv()
         row = row + got_two[peer]
 
@@ -338,11 +336,9 @@
         )
 
     got_three[my_z] = row
-    for step in range(1, size_z):
-        peer, device = z_peer(step)
+    for peer, device in z_peers:
         three_copy(my_z, peer, device).start()
-    for step in range(1, size_z):
-        peer, device = z_peer(step)
+    for peer, device in z_peers:
         three_copy(peer, peer, device).wait_recv()
     row = got_three[0]
     for index in range(1, size_z):
@@ -359,13 +355,11 @@
         )
 
     rows_four[my_y] = row
-    for step in range(1, size_y):
-        peer, device = y_peer(step)
+    for peer, device in y_peers:
         four_copy(my_y, peer, device).start()
 
-    for step in range(1, groups):
-        peer, device = group_peer(step)
-        other = velocities.at[peer // CORES, :, lax.rem(peer, CORES)]
+    for peer, device, peer_x, peer_core in group_peers:
+        other = velocities.at[peer_x, :, peer_core]
         velocity_copy(1, other, (peer, peer), device).wait_recv()
     for at_x in range(size_x):
         for at_y in range(size_y):
@@ -375,34 +369,44 @@
                     at_x, at_y, at_core
                 ]
     bounds = (
-        (0, C_IN, PART_W1[0]),
-        (C_IN, C_IN + 9 * C_MID, PART_W2[0]),
-        (C_IN + 9 * C_MID, K_ROW, PART_W3[0]),
+        (0, C_IN, AT_W1),
+        (C_IN, C_IN + 9 * C_MID, AT_W2),
+        (C_IN + 9 * C_MID, K_ROW, AT_W3),
     )
     weight_norms = [jnp.sqrt(total(params[:, low_end:high_end])) for low_end, high_end, _ in bounds]
 
-    for step in range(1, size_y):
-        peer, device = y_peer(step)
+    for peer, device in y_peers:
         four_copy(peer, peer, device).wait_recv()
     for index in range(size_y):
         grads[my_group, index * own_rows : (index + 1) * own_rows, :] = rows_four[index]
 
-    def five_copy(slot, peer, device):
+    def five_copy(slot, sent, device):
         return pltpu.make_async_remote_copy(
             src_ref=grads.at[slot],
             dst_ref=grads.at[slot],
-            send_sem=send_five.at[peer],
+            send_sem=send_five.at[sent],
             recv_sem=recv_five.at[slot],
             device_id=device,
             device_id_type=MESH,
         )
 
-    for step in range(1, groups):
-        peer, device = group_peer(step)
-        five_copy(my_group, peer, device).start()
-    for step in range(1, groups):
-        peer, device = group_peer(step)
-        five_copy(peer, peer, device).wait_recv()
+    sibling = group_peers[0]
+    same_core = [peer for peer in group_peers[1::2]]
+    far_first = sorted(range(len(same_core)), key=lambda at: -min(at + 1, size_x - 1 - at))
+    for at in far_first:
+        five_copy(my_group, same_core[at][0], same_core[at][1]).start()
+    sent_five = [five_copy(my_group, peer[0], peer[1]) for peer in same_core]
+    own = five_copy(my_group, sibling[0], sibling[1])
+    own.start()
+    sent_five.append(own)
+    for at in far_first[::-1]:
+        slot = same_core[at][0]
+        five_copy(slot, slot, same_core[at][1]).wait_recv()
+        onward = five_copy(slot, group_peers[2 * at + 2][0], sibling[1])
+        onward.start()
+        sent_five.append(onward)
+    for peer in group_peers[::2]:
+        five_copy(peer[0], peer[0], sibling[1]).wait_recv()
 
     for (low_end, high_end, column), weight_norm in zip(bounds, weight_norms):
         grad = grads[:, :, column : column + high_end - low_end].reshape(
@@ -414,21 +418,18 @@
         next_weights[:, low_end:high_end] = params[:, low_end:high_end] - fresh
     new_velocity[...] = velocity_flat[pl.ds(gx * own_rows, own_rows), :]
 
-    for step in range(1, groups):
-        peer, device = group_peer(step)
-        for index in range(3):
-            part_copy(index, parts[index], peer, my_group, device).wait_send()
+    for peer, device, peer_x, peer_core in group_peers:
+        for index in range(len(PARTS)):
+            part_copy(index, PARTS[index], peer, my_group, device).wait_send()
         velocity_copy(1, velocities.at[my_x, :, my_core], (peer, my_group), device).wait_send()
-        five_copy(my_group, peer, device).wait_send()
-    for step in range(1, size_y):
-        peer, device = y_peer(step)
+    for peer, device in y_peers:
         velocity_copy(0, velocities.at[my_x, my_y, my_core], (peer, my_y), device).wait_send()
         two_copy(peer, my_y, device).wait_send()
         four_copy(my_y, peer, device).wait_send()
-    for step in range(1, size_z):
-        peer, device = z_peer(step)
+    for peer, device in z_peers:
         three_copy(my_z, peer, device).wait_send()
-    store.wait()
+    for copy in sent_five:
+        copy.wait_send()
 
 
 def shards(size_x, size_y, size_z, block_input, mid_first, mid_second, out_grad, params, velocity):
@@ -439,23 +440,19 @@
     return pl.pallas_call(
         functools.partial(kernel, size_x, size_y, size_z),
         out_shape=(
-            jax.ShapeDtypeStruct((1, H_DEV, W_IMG, C_IN), BF16),
-            jax.ShapeDtypeStruct((own_rows, K_ROW), F32),
-            jax.ShapeDtypeStruct((C_MID, K_ROW), F32),
+            pltpu.VMEM((1, H_DEV, W_IMG, C_IN), BF16),
+            pltpu.VMEM((own_rows, K_ROW), F32),
+            pltpu.VMEM((C_MID, K_ROW), F32),
         ),
-        in_specs=[pl.BlockSpec(memory_space=pl.ANY)] * 4
-        + [pl.BlockSpec(memory_space=pltpu.VMEM)] * 2,
-        out_specs=(
-            pl.BlockSpec(memory_space=pl.ANY),
-            pl.BlockSpec(memory_space=pltpu.VMEM),
-            pl.BlockSpec(memory_space=pltpu.VMEM),
-        ),
+        in_specs=[pl.BlockSpec(memory_space=pl.ANY)] * 6,
+        out_specs=(pl.BlockSpec(memory_space=pltpu.VMEM),) * 3,
         scratch_shapes=[
             pltpu.VMEM((H_DEV, W_IMG, C_IN), BF16),
             pltpu.VMEM((H_DEV, W_IMG * C_MID), BF16),
             pltpu.VMEM((H_DEV, W_IMG * C_MID), BF16),
             pltpu.VMEM((H_DEV, W_IMG, C_IN), BF16),
-            pltpu.VMEM((H_DEV, W_IMG, C_IN), BF16),
+            pltpu.VMEM((C_MID, K_ROW), F32),
+            pltpu.VMEM((own_rows, K_ROW), F32),
             pltpu.VMEM((PIXELS, 128), F32),
             pltpu.VMEM((PIXELS, 128), F32),
             pltpu.VMEM((PIXELS + 2 * W_PAD, 3 * C_MID), BF16),
@@ -475,10 +472,9 @@
             pltpu.VMEM((groups, group_rows, K_PAD), F32),
             pltpu.VMEM((size_x, size_y, CORES, own_rows, K_ROW), F32),
             pltpu.VMEM((C_MID, K_ROW), F32),
-            dma((4,)),
-            dma,
-            dma((3, groups)),
-            dma((3, groups)),
+            dma((6,)),
+            dma((len(PARTS), groups)),
+            dma((len(PARTS), groups)),
             dma((size_y,)),
             dma((size_y,)),
             dma((size_z,)),

time: 57.4 us -> 48.5 us (0.84)
  Pallas kernels: 52.9 us -> 45.4 us
  local copies, waits for them, and re-layouts: 3.69 us -> 2.31 us
    pallas_call x1, Pallas kernels: 52.9 us -> 45.4 us  [shards(): pl.pallas_call(functools.partial(kernel, size_x, size_y, size_z), out_sha...]
    unnamed x7 -> x3, local copies, waits for them, and re-layouts: 3.69 us -> 2.31 us
where the time goes in v2:
time: 48.5 us; the launch traced here: 48.4 us
  Pallas kernels  45.4 us (94%)
  local copies, waits for them, and re-layouts  2.31 us (5%)
  between operations  0.64 us (1%)
    pallas_call x1, Pallas kernels, shards(): pl.pallas_call(functools.partial(kernel, size_x, size_y, size_z), out_sha...  45.4 us
    unnamed x3, local copies, waits for them, and re-layouts  2.31 us

profile of v2, /device:TPU:1, one launch (start us, length us, event | category | flops | bytes accessed | tf_op | source)
XLA Modules:
  0.0 48.4 jit_solution(11815050524492784210)
XLA Ops:
  0.6 45.4 %bottleneck_backward.1 = (bf16[1,40,56,256]{3,2,1,0:T(8,128)(2,1)S(1)}, f32[1,1088]{1,0:T(1,128)S(1)}, f32[64,1088]{1,0:T(8,128)S(1)}) custom-call(bf16[1,40,56,256]{3,2,1,0:T(8,128)(2,1)} %x_hbm.1, bf16[1,40,3584]{2,1,0:T(8,128)(2,1)} %first_hbm.1, bf16[1,40,3584]{2,1,0:T(8,128)(2,1)} %second_hbm.1, bf16[1,40,56,256]{3,2,1,0:T(8,128)(2,1)} %grad_hbm.1, ...), custom_call_target="tpu_custom_call" | custom-call | tf_op jit(solution)/shard_map/bottleneck_backward/pallas_call | solution.py:440
  46.1 1.0 %copy.12 = bf16[1,40,56,256]{3,2,1,0:T(8,128)(2,1)} copy(bf16[1,40,56,256]{3,2,1,0:T(8,128)(2,1)S(1)} %get-tuple-element.3) | data formatting | bytes 2293760
  47.1 0.6 %copy.13 = f32[1,1088]{1,0:T(1,128)} copy(f32[1,1088]{1,0:T(1,128)S(1)} %get-tuple-element.4) | data formatting | bytes 8704
  47.7 0.7 %copy.14 = f32[64,1088]{1,0:T(8,128)} copy(f32[64,1088]{1,0:T(8,128)S(1)} %get-tuple-element.5) | data formatting | bytes 557056

commit v3 on v2

--- a/solution.py
+++ b/solution.py
@@ -35,7 +35,6 @@
 AT_W3 = 0
 AT_W1 = 256
 AT_W2 = 512
-PARTS = ((0, K_PAD),)
 
 
 def dot(left, right, left_dim, right_dim):
@@ -101,6 +100,8 @@
     sum_two,
     sum_three,
     local,
+    got_pair,
+    pairs,
     got_one,
     rows_two,
     got_two,
@@ -110,6 +111,8 @@
     velocities,
     velocity_flat,
     load_sem,
+    send_pair,
+    recv_pair,
     send_one,
     recv_one,
     send_two,
@@ -163,12 +166,15 @@
         for core in (my_core, 1 - my_core) if step else (1 - my_core,):
             index = (peer_x * size_y + my_y) * CORES + core
             group_peers.append((peer_x * CORES + core, (index, my_z), peer_x, core))
+    def far_first(size):
+        return sorted(range(1, size), key=lambda step: -min(step, size - step))
+
     y_peers = []
-    for step in range(1, size_y):
+    for step in far_first(size_y):
         peer = wrap(my_y + step, size_y)
         y_peers.append((peer, ((my_x * size_y + peer) * CORES + my_core, my_z)))
     z_peers = []
-    for step in range(1, size_z):
+    for step in far_first(size_z):
         peer = wrap(my_z + step, size_z)
         z_peers.append((peer, (gx, peer)))
 
@@ -225,21 +231,31 @@
             groups, group_rows, values.shape[1]
         )
 
-    def part_copy(index, columns, peer, slot, device):
-        return pltpu.make_async_remote_copy(
-            src_ref=local.at[peer, :, pl.ds(*columns)],
-            dst_ref=got_one.at[slot, :, pl.ds(*columns)],
-            send_sem=send_one.at[index, peer],
-            recv_sem=recv_one.at[index, slot],
+    place(AT_W3, sum_three[...] * (scale_three * mean_factor))
+
+    sibling = group_peers[0]
+    same_core = [group_peers[2 * step - 1] for step in far_first(size_x)]
+    other_core = [group_peers[2 * step] for step in far_first(size_x)] + [sibling]
+
+    def pair_copy(at_x, core):
+        return pltpu.make_async_remote_copy(
+            src_ref=local.at[at_x * CORES + core],
+            dst_ref=got_pair.at[at_x],
+            send_sem=send_pair.at[at_x],
+            recv_sem=recv_pair.at[at_x],
+            device_id=sibling[1],
+            device_id_type=MESH,
+        )
+
+    def one_copy(at_x, slot, device):
+        return pltpu.make_async_remote_copy(
+            src_ref=pairs.at[at_x],
+            dst_ref=got_one.at[slot],
+            send_sem=send_one.at[at_x],
+            recv_sem=recv_one.at[slot],
             device_id=device,
             device_id_type=MESH,
         )
-
-    def send_part(index):
-        for peer, device, peer_x, peer_core in group_peers:
-            part_copy(index, PARTS[index], peer, my_group, device).start()
-
-    place(AT_W3, sum_three[...] * (scale_three * mean_factor))
 
     load_first.wait()
     spread_pixels(first_vmem, first_pix)
@@ -281,7 +297,12 @@
     load_velocity.wait()
     velocities[my_x, my_y, my_core] = velocity[...]
     pl.semaphore_wait(barrier, len(everyone))
-    send_part(0)
+    for peer in other_core:
+        pair_copy(peer[2], peer[3]).start()
+    for peer, device, peer_x, peer_core in same_core:
+        pair_copy(peer_x, my_core).wait_recv()
+        pairs[peer_x] = local[peer] + got_pair[peer_x]
+        one_copy(peer_x, my_x, device).start()
     for peer, device in y_peers:
         velocity_copy(0, velocities.at[my_x, my_y, my_core], (peer, my_y), device).start()
 
@@ -294,11 +315,11 @@
 
     each_chunk(step_input)
 
-    block = local[my_group]
-    for peer, device, peer_x, peer_core in group_peers:
-        for index in range(len(PARTS)):
-            part_copy(index, PARTS[index], peer, peer, device).wait_recv()
-        block = block + got_one[peer]
+    pair_copy(my_x, my_core).wait_recv()
+    block = local[my_group] + got_pair[my_x]
+    for peer, device, peer_x, peer_core in same_core[::-1]:
+        one_copy(peer_x, peer_x, device).wait_recv()
+        block = block + got_one[peer_x]
     for index in range(size_y):
         rows_two[index] = block[index * own_rows : (index + 1) * own_rows]
 
@@ -321,7 +342,7 @@
         velocity_copy(1, velocities.at[my_x, :, my_core], (peer, my_group), device).start()
 
     row = rows_two[my_y]
-    for peer, device in y_peers:
+    for peer, device in y_peers[::-1]:
         two_copy(peer, peer, device).wait_recv()
         row = row + got_two[peer]
 
@@ -338,7 +359,7 @@
     got_three[my_z] = row
     for peer, device in z_peers:
         three_copy(my_z, peer, device).start()
-    for peer, device in z_peers:
+    for peer, device in z_peers[::-1]:
         three_copy(peer, peer, device).wait_recv()
     row = got_three[0]
     for index in range(1, size_z):
@@ -375,7 +396,7 @@
     )
     weight_norms = [jnp.sqrt(total(params[:, low_end:high_end])) for low_end, high_end, _ in bounds]
 
-    for peer, device in y_peers:
+    for peer, device in y_peers[::-1]:
         four_copy(peer, peer, device).wait_recv()
     for index in range(size_y):
         grads[my_group, index * own_rows : (index + 1) * own_rows, :] = rows_four[index]
@@ -390,21 +411,19 @@
             device_id_type=MESH,
         )
 
-    sibling = group_peers[0]
-    same_core = [peer for peer in group_peers[1::2]]
-    far_first = sorted(range(len(same_core)), key=lambda at: -min(at + 1, size_x - 1 - at))
-    for at in far_first:
-        five_copy(my_group, same_core[at][0], same_core[at][1]).start()
-    sent_five = [five_copy(my_group, peer[0], peer[1]) for peer in same_core]
-    own = five_copy(my_group, sibling[0], sibling[1])
-    own.start()
-    sent_five.append(own)
-    for at in far_first[::-1]:
-        slot = same_core[at][0]
-        five_copy(slot, slot, same_core[at][1]).wait_recv()
-        onward = five_copy(slot, group_peers[2 * at + 2][0], sibling[1])
-        onward.start()
-        sent_five.append(onward)
+    sent_five = []
+
+    def send_five_to(slot, sent, device):
+        copy = five_copy(slot, sent, device)
+        copy.start()
+        sent_five.append(copy)
+
+    for peer in same_core:
+        send_five_to(my_group, peer[0], peer[1])
+    send_five_to(my_group, sibling[0], sibling[1])
+    for here, there in zip(same_core[::-1], other_core[-2::-1]):
+        five_copy(here[0], here[0], here[1]).wait_recv()
+        send_five_to(here[0], there[0], sibling[1])
     for peer in group_peers[::2]:
         five_copy(peer[0], peer[0], sibling[1]).wait_recv()
 
@@ -419,8 +438,6 @@
     new_velocity[...] = velocity_flat[pl.ds(gx * own_rows, own_rows), :]
 
     for peer, device, peer_x, peer_core in group_peers:
-        for index in range(len(PARTS)):
-            part_copy(index, PARTS[index], peer, my_group, device).wait_send()
         velocity_copy(1, velocities.at[my_x, :, my_core], (peer, my_group), device).wait_send()
     for peer, device in y_peers:
         velocity_copy(0, velocities.at[my_x, my_y, my_core], (peer, my_y), device).wait_send()
@@ -428,6 +445,10 @@
         four_copy(my_y, peer, device).wait_send()
     for peer, device in z_peers:
         three_copy(my_z, peer, device).wait_send()
+    for peer in other_core:
+        pair_copy(peer[2], peer[3]).wait_send()
+    for peer, device, peer_x, peer_core in same_core:
+        one_copy(peer_x, my_x, device).wait_send()
     for copy in sent_five:
         copy.wait_send()
 
@@ -464,7 +485,9 @@
             pltpu.VMEM((3 * C_MID, 3 * C_MID), F32),
             pltpu.VMEM((C_MID, C_IN), F32),
             pltpu.VMEM((groups, group_rows, K_PAD), F32),
-            pltpu.VMEM((groups, group_rows, K_PAD), F32),
+            pltpu.VMEM((size_x, group_rows, K_PAD), F32),
+            pltpu.VMEM((size_x, group_rows, K_PAD), F32),
+            pltpu.VMEM((size_x, group_rows, K_PAD), F32),
             pltpu.VMEM((size_y, own_rows, K_PAD), F32),
             pltpu.VMEM((size_y, own_rows, K_PAD), F32),
             pltpu.VMEM((size_z, own_rows, K_PAD), F32),
@@ -473,8 +496,10 @@
             pltpu.VMEM((size_x, size_y, CORES, own_rows, K_ROW), F32),
             pltpu.VMEM((C_MID, K_ROW), F32),
             dma((6,)),
-            dma((len(PARTS), groups)),
-            dma((len(PARTS), groups)),
+            dma((size_x,)),
+            dma((size_x,)),
+            dma((size_x,)),
+            dma((size_x,)),
             dma((size_y,)),
             dma((size_y,)),
             dma((size_z,)),

time: 48.5 us -> 48.4 us (level)
  no operation moved by 1% of the time
where the time goes in v3:
time: 48.4 us; the launch traced here: 48.2 us
  Pallas kernels  45.3 us (94%)
  local copies, waits for them, and re-layouts  2.31 us (5%)
  between operations  0.64 us (1%)
    pallas_call x1, Pallas kernels, shards(): pl.pallas_call(functools.partial(kernel, size_x, size_y, size_z), out_sha...  45.3 us
    unnamed x3, local copies, waits for them, and re-layouts  2.31 us

profile of v3, /device:TPU:1, one launch (start us, length us, event | category | flops | bytes accessed | tf_op | source)
XLA Modules:
  0.0 48.2 jit_solution(871037554109989007)
XLA Ops:
  0.6 45.3 %bottleneck_backward.1 = (bf16[1,40,56,256]{3,2,1,0:T(8,128)(2,1)S(1)}, f32[1,1088]{1,0:T(1,128)S(1)}, f32[64,1088]{1,0:T(8,128)S(1)}) custom-call(bf16[1,40,56,256]{3,2,1,0:T(8,128)(2,1)} %x_hbm.1, bf16[1,40,3584]{2,1,0:T(8,128)(2,1)} %first_hbm.1, bf16[1,40,3584]{2,1,0:T(8,128)(2,1)} %second_hbm.1, bf16[1,40,56,256]{3,2,1,0:T(8,128)(2,1)} %grad_hbm.1, ...), custom_call_target="tpu_custom_call" | custom-call | tf_op jit(solution)/shard_map/bottleneck_backward/pallas_call | solution.py:461
  45.9 1.0 %copy.12 = bf16[1,40,56,256]{3,2,1,0:T(8,128)(2,1)} copy(bf16[1,40,56,256]{3,2,1,0:T(8,128)(2,1)S(1)} %get-tuple-element.3) | data formatting | bytes 2293760
  46.9 0.6 %copy.13 = f32[1,1088]{1,0:T(1,128)} copy(f32[1,1088]{1,0:T(1,128)S(1)} %get-tuple-element.4) | data formatting | bytes 8704
  47.5 0.7 %copy.14 = f32[64,1088]{1,0:T(8,128)} copy(f32[64,1088]{1,0:T(8,128)S(1)} %get-tuple-element.5) | data formatting | bytes 557056

commit v4 on v3

--- a/solution.py
+++ b/solution.py
@@ -20,7 +20,7 @@
 ROWS_Y = 8
 CORES = 2
 
-H_CHUNK = 8
+H_CHUNK = 40
 CHUNK = H_CHUNK * W_PAD
 CHUNKS = H_DEV // H_CHUNK
 
@@ -179,7 +179,7 @@
         z_peers.append((peer, (gx, peer)))
 
     barrier = pltpu.get_barrier_semaphore()
-    everyone = [peer[1] for peer in group_peers + y_peers + z_peers]
+    everyone = [peer[1] for peer in z_peers + y_peers + group_peers]
     for device in everyone:
         pl.semaphore_signal(barrier, inc=1, device_id=device, device_id_type=MESH)
 

time: 48.4 us -> 48.1 us (level)
  no operation moved by 1% of the time
where the time goes in v4:
time: 48.1 us; the launch traced here: 47.9 us
  Pallas kernels  45 us (94%)
  local copies, waits for them, and re-layouts  2.31 us (5%)
  between operations  0.64 us (1%)
    pallas_call x1, Pallas kernels, shards(): pl.pallas_call(functools.partial(kernel, size_x, size_y, size_z), out_sha...  45 us
    unnamed x3, local copies, waits for them, and re-layouts  2.31 us

profile of v4, /device:TPU:1, one launch (start us, length us, event | category | flops | bytes accessed | tf_op | source)
XLA Modules:
  0.0 47.9 jit_solution(16537073694178647771)
XLA Ops:
  0.6 45.0 %bottleneck_backward.1 = (bf16[1,40,56,256]{3,2,1,0:T(8,128)(2,1)S(1)}, f32[1,1088]{1,0:T(1,128)S(1)}, f32[64,1088]{1,0:T(8,128)S(1)}) custom-call(bf16[1,40,56,256]{3,2,1,0:T(8,128)(2,1)} %x_hbm.1, bf16[1,40,3584]{2,1,0:T(8,128)(2,1)} %first_hbm.1, bf16[1,40,3584]{2,1,0:T(8,128)(2,1)} %second_hbm.1, bf16[1,40,56,256]{3,2,1,0:T(8,128)(2,1)} %grad_hbm.1, ...), custom_call_target="tpu_custom_call" | custom-call | tf_op jit(solution)/shard_map/bottleneck_backward/pallas_call | solution.py:461
  45.6 1.0 %copy.12 = bf16[1,40,56,256]{3,2,1,0:T(8,128)(2,1)} copy(bf16[1,40,56,256]{3,2,1,0:T(8,128)(2,1)S(1)} %get-tuple-element.3) | data formatting | bytes 2293760
  46.6 0.6 %copy.13 = f32[1,1088]{1,0:T(1,128)} copy(f32[1,1088]{1,0:T(1,128)S(1)} %get-tuple-element.4) | data formatting | bytes 8704
  47.2 0.7 %copy.14 = f32[64,1088]{1,0:T(8,128)} copy(f32[64,1088]{1,0:T(8,128)S(1)} %get-tuple-element.5) | data formatting | bytes 557056
